TPU v7x, 512 devices: a whole 4x4x16 slice. The times are simulated.
512 devices in a mesh: expert: 128 (over z, y, core), dp: 4 (over x).
Axes of the slice: x: 4, y: 4, z: 16, core: 2. Of those that a mesh axis runs over, the one named last changes fastest.
Arguments:
- tokens: bfloat16 [16384, 2048], P('expert', 'dp'), may hold values from -6 to 6
- grad_out: bfloat16 [16384, 2048], P('expert', 'dp'), may hold values from -6 to 6
- routes: int32 [16384, 8], P('expert'), may hold values from 0 to 127, all different within a row; in each aligned block of 128 rows (0 to 127, 128 to 255, ...) at most 12 rows name the same one
- gates: float32 [16384, 8], P('expert'), may hold values from 0.1 to 1
- w_gate: bfloat16 [128, 2048, 384], P('expert', 'dp'), may hold values from -0.125 to 0.125
- w_up: bfloat16 [128, 2048, 384], P('expert', 'dp'), may hold values from -0.125 to 0.125
- w_down: bfloat16 [128, 384, 2048], P('expert', None, 'dp'), may hold values from -0.3125 to 0.3125
Outputs:
- d_tokens: bfloat16 [16384, 2048], P('expert', 'dp')
- grad_gate: bfloat16 [128, 2048, 384], P('expert', 'dp')
- grad_up: bfloat16 [128, 2048, 384], P('expert', 'dp')
- grad_down: bfloat16 [128, 384, 2048], P('expert', None, 'dp')
Inputs may be any that keep to these rules, and one draw needn't show every extreme that they name: `routes`: each row names 8 different experts; in each aligned block of 128 rows no expert is named by more than 12 rows, a bound that some block reaches.
All inputs are finite; a program needn't handle non-finite values.
Results may differ from a plain program's by a relative error of at most 0.013.
Values may be sent and summed in bfloat16 or wider, within the bound.
No kernel may reach another device: no remote copies, remote signals or barrier semaphores. Data moves between devices by JAX's collectives and lax.ppermute only.
A program may use at most 64 MiB of HBM per device.

v0:
```python
import jax
import jax.numpy as jnp
from jax import lax
from jax.sharding import Mesh
from jax.sharding import PartitionSpec as P

MOST = 12
N_Z, N_Y, N_C, N_X = (16, 4, 2, 4)
PLANE = ("x", "y", "c")
F32 = jnp.float32
BF16 = jnp.bfloat16


def dot(left, right, contract, batch=((), ())):
    return lax.dot_general(left, right, (contract, batch), preferred_element_type=F32)


def shift(value, by):
    return lax.ppermute(value, "x", [(i, (i + by) % N_X) for i in range(N_X)])


def gather_x(value, me):
    whole = jnp.zeros((N_X,) + value.shape, value.dtype)
    for by in range(N_X):
        piece = value if by == 0 else shift(value, by)
        whole = lax.dynamic_update_slice_in_dim(whole, piece[None], (me - by) % N_X, 0)
    return whole


def plan(routes, gates, me_z):
    tok = routes.shape[0]
    mine = jnp.concatenate([routes.T.astype(F32), gates.T], axis=0)
    every = lax.all_to_all(
        jnp.broadcast_to(mine[None], (N_Z,) + mine.shape),
        "z",
        split_axis=0,
        concat_axis=0,
        tiled=True,
    )
    top = routes.shape[1]
    near = N_Y * N_C
    named = every[:, :top].reshape(N_Z, top, 1, tok)
    weight = every[:, top:].reshape(N_Z, top, 1, tok)
    wanted = (me_z * near + jnp.arange(near, dtype=jnp.int32)).astype(F32)
    hit = named == wanted[None, None, :, None]
    member = jnp.sum(hit.astype(F32), axis=1)
    gate = jnp.sum(jnp.where(hit, weight, 0.0), axis=1)
    before = (jnp.arange(tok)[:, None] < jnp.arange(tok)[None, :]).astype(BF16)
    rank = dot(member.astype(BF16), before, ((2,), (0,)))
    within = (jnp.arange(N_Z) % (N_Z // N_X) * MOST).astype(F32)
    slot = jnp.where(member > 0.5, rank + within[:, None, None], -1.0)

    def by_group(value):
        value = value.reshape(N_X, N_Z // N_X, near, tok)
        return value.transpose(0, 2, 1, 3).reshape(N_X, near, 1, N_Z // N_X * tok)

    slots = N_Z // N_X * MOST
    pick = by_group(slot) == jnp.arange(slots, dtype=jnp.int32).astype(F32)[None, None, :, None]
    row_gate = jnp.sum(jnp.where(pick, by_group(gate), 0.0), axis=3)
    return (
        pick.astype(BF16).reshape(N_X, near * slots, N_Z // N_X * tok),
        row_gate.reshape(N_X, near * slots, 1),
    )


def shards(tokens, grad_out, routes, gates, w_gate, w_up, w_down):
    me_z, me_x = (lax.axis_index("z"), lax.axis_index("x"))
    tok, cols = tokens.shape
    both = jnp.concatenate([tokens, grad_out], axis=1)
    column = lax.all_gather(both, "z", axis=0, tiled=True).reshape(N_X, N_Z // N_X * tok, 2 * cols)
    pick, row_gate = plan(routes, gates, me_z)
    full_gate = gather_x(w_gate[0], me_x)
    full_up = gather_x(w_up[0], me_x)
    full_down = gather_x(w_down[0], me_x)
    rows = dot(pick, column, ((2,), (1,)), ((0,), (0,)))
    scale = jnp.where(jnp.arange(2 * cols)[None, None, :] < cols, 1.0, row_gate)
    rows = (rows * scale).astype(BF16)
    count = rows.shape[1]
    slots = count // (N_Y * N_C)
    rows = lax.all_to_all(
        rows.reshape(-1, slots, 2 * cols), PLANE, split_axis=0, concat_axis=0, tiled=True
    ).reshape(N_X, count, 2 * cols)
    inputs, scaled = (rows[:, :, :cols], rows[:, :, cols:])

    def over_features(left, right, axis):
        return sum((dot(left[j], right[j], ((1,), (axis,))) for j in range(N_X)))

    pre_gate = over_features(inputs, full_gate, 0)
    pre_up = over_features(inputs, full_up, 0)
    back_hidden = over_features(scaled, full_down, 1)
    sigmoid_gate = jax.nn.sigmoid(pre_gate)
    activated = pre_gate * sigmoid_gate
    hidden = (activated * pre_up).astype(BF16)
    d_up = (back_hidden * activated).astype(BF16)
    d_gate = (back_hidden * pre_up * sigmoid_gate * (1.0 + pre_gate * (1.0 - sigmoid_gate))).astype(
        BF16
    )
    row_grad = jnp.stack(
        [
            (dot(d_gate, full_gate[j], ((1,), (1,))) + dot(d_up, full_up[j], ((1,), (1,)))).astype(
                BF16
            )
            for j in range(N_X)
        ]
    )
    came_back = lax.all_to_all(
        row_grad.reshape(-1, slots, cols), PLANE, split_axis=0, concat_axis=0, tiled=True
    ).reshape(N_X, count, cols)
    token_grad = dot(pick, came_back, ((1,), (1,)), ((0,), (0,))).astype(BF16)
    d_tokens = lax.psum_scatter(token_grad.reshape(-1, cols), "z", scatter_dimension=0, tiled=True)
    totals = [None, None, None]
    for by in (1, 3, 2, 0):
        to = (me_x + by) % N_X
        ins = lax.dynamic_index_in_dim(inputs, to, 0, keepdims=False)
        outs = lax.dynamic_index_in_dim(scaled, to, 0, keepdims=False)
        for k, (left, right) in enumerate(((ins, d_gate), (ins, d_up), (hidden, outs))):
            part = dot(left, right, ((0,), (0,))).astype(BF16)
            part = (shift(part, by) if by else part).astype(F32)
            totals[k] = part if totals[k] is None else totals[k] + part
    grads = [total.astype(BF16)[None] for total in totals]
    return (d_tokens, *grads)


def solution(mesh):
    fine = Mesh(mesh.devices.reshape(N_Z, N_Y, N_C, N_X), ("z", "y", "c", "x"))
    expert = ("z", "y", "c")
    return jax.shard_map(
        shards,
        mesh=fine,
        in_specs=(
            P(expert, "x"),
            P(expert, "x"),
            P(expert, None),
            P(expert, None),
            P(expert, "x", None),
            P(expert, "x", None),
            P(expert, None, "x"),
        ),
        out_specs=(
            P(expert, "x"),
            P(expert, "x", None),
            P(expert, "x", None),
            P(expert, None, "x"),
        ),
        check_vma=False,
    )
```

profile of v0, /device:TPU:4, one launch (start us, length us, event | category | flops | bytes accessed | tf_op | source)
XLA Modules:
  0.0 332.0 jit_solution(9735553200323661937)
XLA Ops:
  11.0 15.2 %all-to-all-start = ((f32[16,16,128]{2,1,0:T(8,128)}), f32[16,16,128]{2,1,0:T(8,128)S(1)}, u32[]{:S(2)}, u32[]{:S(2)}) async-start(f32[16,16,128]{2,1,0:T(8,128)} %broadcast_in_dim.103), calls=%async_computation | async-start | bytes 262144 | tf_op jit(solution)/shard_map/all_to_all | solution.py:33
  26.3 14.6 %all-to-all-done = f32[16,16,128]{2,1,0:T(8,128)S(1)} async-done(((f32[16,16,128]{2,1,0:T(8,128)}), f32[16,16,128]{2,1,0:T(8,128)S(1)}, u32[]{:S(2)}, u32[]{:S(2)}) %all-to-all-start) | async-done | bytes 131104 | tf_op jit(solution)/shard_map/all_to_all | solution.py:33
  42.3 52.2 %all-gather.2.cloned.1.call-done = bf16[2048,1024]{1,0:T(8,128)(2,1)} async-done(((bf16[128,1024]{1,0:T(8,128)(2,1)}), bf16[2048,1024]{1,0:T(8,128)(2,1)}) %all-gather.2.cloned.1.call-update) | async-done | bytes 4194320 | tf_op jit(solution)/shard_map/all_gather | solution.py:70
  94.4 5.6 %multiply_convert_fusion = bf16[4,384,1024]{2,1,0:T(8,128)(2,1)} fusion(f32[4,384]{1,0:T(4,128)S(1)} %broadcast_in_dim.112, pred[1024]{0:T(1024)(128)(4,1)S(1)} %iota_compare_fusion.1, pred[4,384,512]{2,1,0:T(32,128)(4,1)S(1)} %bitcast_compare_fusion, bf16[4,512,1024]{2,1,0:T(8,128)(2,1)} %bitcast.227), kind=kOutput, calls=%fused_computation | convolution fusion | flops 1615331328 | bytes 8133632 | tf_op jit(solution)/shard_map/dot_general | solution.py:15
  100.1 7.6 %all-to-all-start.1 = ((bf16[32,48,1024]{2,1,0:T(8,128)(2,1)}), bf16[32,48,1024]{2,1,0:T(8,128)(2,1)S(1)}, u32[]{:S(2)}, u32[]{:S(2)}) async-start(bf16[32,48,1024]{2,1,0:T(8,128)(2,1)} %bitcast.213), calls=%async_computation.1 | async-start | bytes 6291456 | tf_op jit(solution)/shard_map/all_to_all | solution.py:80
  107.7 3.1 collective-permute-start.6
  110.9 2.7 collective-permute-start.7
  113.6 2.7 collective-permute-start.8
  116.3 3.2 collective-permute-start
  119.5 4.6 %collective-permute-start.1 = (bf16[384,512]{1,0:T(8,128)(2,1)}, bf16[384,512]{1,0:T(8,128)(2,1)}, u32[]{:S(2)}, u32[]{:S(2)}) collective-permute-start(bf16[384,512]{1,0:T(8,128)(2,1)} %bitcast.220), channel_id=1, source_target_pairs={{0,2},{1,3},{2,0},{3,1},{4,6},{5,7},{6,4},{7,5},{8,10},{9,11},{10,... | collective-permute-start | bytes 1179656 | tf_op jit(solution)/shard_map/ppermute | solution.py:19
  130.5 22.3 %collective-permute-done.6 = bf16[512,384]{1,0:T(8,128)(2,1)} collective-permute-done((bf16[512,384]{1,0:T(8,128)(2,1)S(1)}, bf16[512,384]{1,0:T(8,128)(2,1)}, u32[]{:S(2)}, u32[]{:S(2)}) %collective-permute-start.6) | collective-permute-done | bytes 393248 | tf_op jit(solution)/shard_map/ppermute | solution.py:19
  152.8 2.7 collective-permute-start.2
  157.3 12.5 %collective-permute-done = bf16[384,512]{1,0:T(8,128)(2,1)} collective-permute-done((bf16[384,512]{1,0:T(8,128)(2,1)}, bf16[384,512]{1,0:T(8,128)(2,1)}, u32[]{:S(2)}, u32[]{:S(2)}) %collective-permute-start) | collective-permute-done | bytes 393248 | tf_op jit(solution)/shard_map/ppermute | solution.py:19
  169.8 4.4 %collective-permute-start.3 = (bf16[512,384]{1,0:T(8,128)(2,1)S(1)}, bf16[512,384]{1,0:T(8,128)(2,1)S(1)}, u32[]{:S(2)}, u32[]{:S(2)}) collective-permute-start(bf16[512,384]{1,0:T(8,128)(2,1)S(1)} %bitcast.222), channel_id=1, source_target_pairs={{0,1},{1,2},{2,3},{3,0},{4,5},{5,6},{6,7},{7,4},{8,9},{9,10},{10,1... | collective-permute-start | bytes 1179656 | tf_op jit(solution)/shard_map/ppermute | solution.py:19
  176.0 1.9 collective-permute-start.4
  179.7 3.4 %collective-permute-start.5 = (bf16[512,384]{1,0:T(8,128)(2,1)S(1)}, bf16[512,384]{1,0:T(8,128)(2,1)S(1)}, u32[]{:S(2)}, u32[]{:S(2)}) collective-permute-start(bf16[512,384]{1,0:T(8,128)(2,1)S(1)} %bitcast.224), channel_id=1, source_target_pairs={{0,3},{1,0},{2,1},{3,2},{4,7},{5,4},{6,5},{7,6},{8,11},{9,8},{10,9... | collective-permute-start | bytes 1179656 | tf_op jit(solution)/shard_map/ppermute | solution.py:19
  188.2 6.6 %collective-permute-done.4 = bf16[512,384]{1,0:T(8,128)(2,1)S(1)} collective-permute-done((bf16[512,384]{1,0:T(8,128)(2,1)S(1)}, bf16[512,384]{1,0:T(8,128)(2,1)S(1)}, u32[]{:S(2)}, u32[]{:S(2)}) %collective-permute-start.4) | collective-permute-done | bytes 393248 | tf_op jit(solution)/shard_map/ppermute | solution.py:19
  211.8 2.3 multiply_convert_fusion.1
  225.6 29.2 %all_to_all.15 = bf16[32,48,512]{2,1,0:T(8,128)(2,1)S(1)} all-to-all(bf16[32,48,512]{2,1,0:T(8,128)(2,1)S(1)} %bitcast.211), channel_id=1, replica_groups=mesh['z'=16,'y'=4,'c'=2,'x'=4] {'x','y','c'}, dimensions={0} | all-to-all | bytes 3145728 | tf_op jit(solution)/shard_map/all_to_all | solution.py:106
  254.7 2.6 convolution_convert_fusion
  258.2 3.7 %collective-permute-start.11 = (bf16[512,384]{1,0:T(8,128)(2,1)S(1)}, bf16[512,384]{1,0:T(8,128)(2,1)S(1)}, u32[]{:S(2)}, u32[]{:S(2)}) collective-permute-start(bf16[512,384]{1,0:T(8,128)(2,1)S(1)} %convolution_convert_fusion.10), channel_id=1, source_target_pairs={{0,2},{1,3},{2,0},{3,1},{4,6},{5,7},{6,4},{7,5},{8,10},{9,11},{10,... | collective-permute-start | bytes 1179656 | tf_op jit(solution)/shard_map/ppermute | solution.py:19
  262.4 2.5 collective-permute-start.10
  265.3 4.5 %collective-permute-start.17 = (bf16[384,512]{1,0:T(8,128)(2,1)S(1)}, bf16[384,512]{1,0:T(8,128)(2,1)S(1)}, u32[]{:S(2)}, u32[]{:S(2)}) collective-permute-start(bf16[384,512]{1,0:T(8,128)(2,1)S(1)} %convolution_convert_fusion.2), channel_id=1, source_target_pairs={{0,2},{1,3},{2,0},{3,1},{4,6},{5,7},{6,4},{7,5},{8,10},{9,11},{10,... | collective-permute-start | bytes 1179656 | tf_op jit(solution)/shard_map/ppermute | solution.py:19
  270.2 2.4 collective-permute-start.16
  273.0 3.5 %collective-permute-start.15 = (bf16[384,512]{1,0:T(8,128)(2,1)S(1)}, bf16[384,512]{1,0:T(8,128)(2,1)S(1)}, u32[]{:S(2)}, u32[]{:S(2)}) collective-permute-start(bf16[384,512]{1,0:T(8,128)(2,1)S(1)} %convolution_convert_fusion.4), channel_id=1, source_target_pairs={{0,1},{1,2},{2,3},{3,0},{4,5},{5,6},{6,7},{7,4},{8,9},{9,10},{10,1... | collective-permute-start | bytes 1179656 | tf_op jit(solution)/shard_map/ppermute | solution.py:19
  277.8 4.4 %collective-permute-start.9 = (bf16[512,384]{1,0:T(8,128)(2,1)S(1)}, bf16[512,384]{1,0:T(8,128)(2,1)S(1)}, u32[]{:S(2)}, u32[]{:S(2)}) collective-permute-start(bf16[512,384]{1,0:T(8,128)(2,1)S(1)} %convolution_convert_fusion.12), channel_id=1, source_target_pairs={{0,1},{1,2},{2,3},{3,0},{4,5},{5,6},{6,7},{7,4},{8,9},{9,10},{10,1... | collective-permute-start | bytes 1179656 | tf_op jit(solution)/shard_map/ppermute | solution.py:19
  282.8 3.0 collective-permute-start.14
  285.8 12.4 %collective-permute-done.16 = bf16[384,512]{1,0:T(8,128)(2,1)S(1)} collective-permute-done((bf16[384,512]{1,0:T(8,128)(2,1)S(1)}, bf16[384,512]{1,0:T(8,128)(2,1)S(1)}, u32[]{:S(2)}, u32[]{:S(2)}) %collective-permute-start.16) | collective-permute-done | bytes 393248 | tf_op jit(solution)/shard_map/ppermute | solution.py:19
  298.2 3.2 collective-permute-start.13
  301.4 2.6 collective-permute-start.12
  307.2 7.7 %collective-permute-done.13 = bf16[512,384]{1,0:T(8,128)(2,1)S(1)} collective-permute-done((bf16[512,384]{1,0:T(8,128)(2,1)S(1)}, bf16[512,384]{1,0:T(8,128)(2,1)S(1)}, u32[]{:S(2)}, u32[]{:S(2)}) %collective-permute-start.13) | collective-permute-done | bytes 393248 | tf_op jit(solution)/shard_map/ppermute | solution.py:19
  316.4 8.7 %reduce-scatter.2.cloned.1.call-done = bf16[128,512]{1,0:T(8,128)(2,1)} async-done(((bf16[2048,512]{1,0:T(8,128)(2,1)}), bf16[128,512]{1,0:T(8,128)(2,1)}) %reduce-scatter.2.cloned.1.call-update) | async-done | bytes 131088 | tf_op jit(solution)/shard_map/reduce_scatter | solution.py:110
  (100 shorter events, 59.4 us)
Async XLA Ops:
  7.2 87.3 %all-gather.2.cloned.1.call-start = ((), (), s32[]{:S(2)}) async-start(), calls=%async_computation.4 | async-start | bytes 4456448 | tf_op jit(solution)/shard_map/all_gather | solution.py:70
  11.0 29.9 %all-to-all-start = ((f32[16,16,128]{2,1,0:T(8,128)}), f32[16,16,128]{2,1,0:T(8,128)S(1)}, u32[]{:S(2)}, u32[]{:S(2)}) async-start(f32[16,16,128]{2,1,0:T(8,128)} %broadcast_in_dim.103), calls=%async_computation | async-start | bytes 262144 | tf_op jit(solution)/shard_map/all_to_all | solution.py:33
  41.7 58.3 %copy-start.3 = (pred[4,384,512]{2,1,0:T(32,128)(4,1)}, pred[4,384,512]{2,1,0:T(32,128)(4,1)S(1)}, u32[]{:S(2)}) copy-start(pred[4,384,512]{2,1,0:T(32,128)(4,1)S(1)} %bitcast_compare_fusion) | copy-start | bytes 2359300
  100.1 7.7 %copy-start.5 = (bf16[1,512,384]{2,1,0:T(8,128)(2,1)S(1)}, bf16[1,512,384]{2,1,0:T(8,128)(2,1)}, u32[]{:S(2)}) copy-start(bf16[1,512,384]{2,1,0:T(8,128)(2,1)} %param.11) | copy-start | bytes 1179652
  100.1 96.6 %all-to-all-start.1 = ((bf16[32,48,1024]{2,1,0:T(8,128)(2,1)}), bf16[32,48,1024]{2,1,0:T(8,128)(2,1)S(1)}, u32[]{:S(2)}, u32[]{:S(2)}) async-start(bf16[32,48,1024]{2,1,0:T(8,128)(2,1)} %bitcast.213), calls=%async_computation.1 | async-start | bytes 6291456 | tf_op jit(solution)/shard_map/all_to_all | solution.py:80
  107.7 217.5 %reduce-scatter.2.cloned.1.call-start = ((), (), s32[]{:S(2)}) async-start(), calls=%async_computation.5 | async-start | bytes 2228224 | tf_op jit(solution)/shard_map/reduce_scatter | solution.py:110
  107.7 45.1 %collective-permute-start.6 = (bf16[512,384]{1,0:T(8,128)(2,1)S(1)}, bf16[512,384]{1,0:T(8,128)(2,1)}, u32[]{:S(2)}, u32[]{:S(2)}) collective-permute-start(bf16[512,384]{1,0:T(8,128)(2,1)S(1)} %bitcast.216), channel_id=1, source_target_pairs={{0,1},{1,2},{2,3},{3,0},{4,5},{5,6},{6,7},{7,4},{8,9},{9,10},{10,1... | collective-permute-start | bytes 1179656 | tf_op jit(solution)/shard_map/ppermute | solution.py:19
  110.9 65.1 %collective-permute-start.7 = (bf16[512,384]{1,0:T(8,128)(2,1)S(1)}, bf16[512,384]{1,0:T(8,128)(2,1)}, u32[]{:S(2)}, u32[]{:S(2)}) collective-permute-start(bf16[512,384]{1,0:T(8,128)(2,1)S(1)} %bitcast.217), channel_id=1, source_target_pairs={{0,2},{1,3},{2,0},{3,1},{4,6},{5,7},{6,4},{7,5},{8,10},{9,11},{10,... | collective-permute-start | bytes 1179656 | tf_op jit(solution)/shard_map/ppermute | solution.py:19
  113.6 71.3 %collective-permute-start.8 = (bf16[512,384]{1,0:T(8,128)(2,1)S(1)}, bf16[512,384]{1,0:T(8,128)(2,1)}, u32[]{:S(2)}, u32[]{:S(2)}) collective-permute-start(bf16[512,384]{1,0:T(8,128)(2,1)S(1)} %bitcast.218), channel_id=1, source_target_pairs={{0,3},{1,0},{2,1},{3,2},{4,7},{5,4},{6,5},{7,6},{8,11},{9,8},{10,9... | collective-permute-start | bytes 1179656 | tf_op jit(solution)/shard_map/ppermute | solution.py:19
  116.3 53.5 %collective-permute-start = (bf16[384,512]{1,0:T(8,128)(2,1)}, bf16[384,512]{1,0:T(8,128)(2,1)}, u32[]{:S(2)}, u32[]{:S(2)}) collective-permute-start(bf16[384,512]{1,0:T(8,128)(2,1)} %bitcast.219), channel_id=1, source_target_pairs={{0,1},{1,2},{2,3},{3,0},{4,5},{5,6},{6,7},{7,4},{8,9},{9,10},{10,1... | collective-permute-start | bytes 1179656 | tf_op jit(solution)/shard_map/ppermute | solution.py:19
  119.5 60.2 %collective-permute-start.1 = (bf16[384,512]{1,0:T(8,128)(2,1)}, bf16[384,512]{1,0:T(8,128)(2,1)}, u32[]{:S(2)}, u32[]{:S(2)}) collective-permute-start(bf16[384,512]{1,0:T(8,128)(2,1)} %bitcast.220), channel_id=1, source_target_pairs={{0,2},{1,3},{2,0},{3,1},{4,6},{5,7},{6,4},{7,5},{8,10},{9,11},{10,... | collective-permute-start | bytes 1179656 | tf_op jit(solution)/shard_map/ppermute | solution.py:19
  125.4 2.1 copy-start.6
  128.3 1.4 copy-start.8
  128.3 24.5 %copy-start.7 = (bf16[1,384,512]{2,1,0:T(8,128)(2,1)S(1)}, bf16[1,384,512]{2,1,0:T(8,128)(2,1)}, u32[]{:S(2)}) copy-start(bf16[1,384,512]{2,1,0:T(8,128)(2,1)} %param.13) | copy-start | bytes 1179652
  152.8 33.8 %collective-permute-start.2 = (bf16[384,512]{1,0:T(8,128)(2,1)S(1)}, bf16[384,512]{1,0:T(8,128)(2,1)S(1)}, u32[]{:S(2)}, u32[]{:S(2)}) collective-permute-start(bf16[384,512]{1,0:T(8,128)(2,1)S(1)} %bitcast.221), channel_id=1, source_target_pairs={{0,3},{1,0},{2,1},{3,2},{4,7},{5,4},{6,5},{7,6},{8,11},{9,8},{10,9... | collective-permute-start | bytes 1179656 | tf_op jit(solution)/shard_map/ppermute | solution.py:19
  169.8 17.6 %collective-permute-start.3 = (bf16[512,384]{1,0:T(8,128)(2,1)S(1)}, bf16[512,384]{1,0:T(8,128)(2,1)S(1)}, u32[]{:S(2)}, u32[]{:S(2)}) collective-permute-start(bf16[512,384]{1,0:T(8,128)(2,1)S(1)} %bitcast.222), channel_id=1, source_target_pairs={{0,1},{1,2},{2,3},{3,0},{4,5},{5,6},{6,7},{7,4},{8,9},{9,10},{10,1... | collective-permute-start | bytes 1179656 | tf_op jit(solution)/shard_map/ppermute | solution.py:19
  176.0 18.9 %collective-permute-start.4 = (bf16[512,384]{1,0:T(8,128)(2,1)S(1)}, bf16[512,384]{1,0:T(8,128)(2,1)S(1)}, u32[]{:S(2)}, u32[]{:S(2)}) collective-permute-start(bf16[512,384]{1,0:T(8,128)(2,1)S(1)} %bitcast.223), channel_id=1, source_target_pairs={{0,2},{1,3},{2,0},{3,1},{4,6},{5,7},{6,4},{7,5},{8,10},{9,11},{10,... | collective-permute-start | bytes 1179656 | tf_op jit(solution)/shard_map/ppermute | solution.py:19
  179.7 16.1 %collective-permute-start.5 = (bf16[512,384]{1,0:T(8,128)(2,1)S(1)}, bf16[512,384]{1,0:T(8,128)(2,1)S(1)}, u32[]{:S(2)}, u32[]{:S(2)}) collective-permute-start(bf16[512,384]{1,0:T(8,128)(2,1)S(1)} %bitcast.224), channel_id=1, source_target_pairs={{0,3},{1,0},{2,1},{3,2},{4,7},{5,4},{6,5},{7,6},{8,11},{9,8},{10,9... | collective-permute-start | bytes 1179656 | tf_op jit(solution)/shard_map/ppermute | solution.py:19
  214.0 4.3 %copy-start = (bf16[384,384]{1,0:T(8,128)(2,1)}, bf16[384,384]{1,0:T(8,128)(2,1)S(1)}, u32[]{:S(2)}) copy-start(bf16[384,384]{1,0:T(8,128)(2,1)S(1)} %get-tuple-element.10) | copy-start | bytes 884740
  225.6 29.2 %copy-start.4 = (pred[4,384,512]{2,1,0:T(32,128)(4,1)S(1)}, pred[4,384,512]{2,1,0:T(32,128)(4,1)}, u32[]{:S(2)}) copy-start(pred[4,384,512]{2,1,0:T(32,128)(4,1)} %copy-done.3) | copy-start | bytes 2359300
  257.7 7.2 %copy-start.2 = (bf16[384,384]{1,0:T(8,128)(2,1)S(1)}, bf16[384,384]{1,0:T(8,128)(2,1)}, u32[]{:S(2)}) copy-start(bf16[384,384]{1,0:T(8,128)(2,1)} %get-tuple-element.8) | copy-start | bytes 884740
  258.2 19.7 %collective-permute-start.11 = (bf16[512,384]{1,0:T(8,128)(2,1)S(1)}, bf16[512,384]{1,0:T(8,128)(2,1)S(1)}, u32[]{:S(2)}, u32[]{:S(2)}) collective-permute-start(bf16[512,384]{1,0:T(8,128)(2,1)S(1)} %convolution_convert_fusion.10), channel_id=1, source_target_pairs={{0,2},{1,3},{2,0},{3,1},{4,6},{5,7},{6,4},{7,5},{8,10},{9,11},{10,... | collective-permute-start | bytes 1179656 | tf_op jit(solution)/shard_map/ppermute | solution.py:19
  262.4 42.8 %collective-permute-start.10 = (bf16[512,384]{1,0:T(8,128)(2,1)S(1)}, bf16[512,384]{1,0:T(8,128)(2,1)S(1)}, u32[]{:S(2)}, u32[]{:S(2)}) collective-permute-start(bf16[512,384]{1,0:T(8,128)(2,1)S(1)} %convolution_convert_fusion.11), channel_id=1, source_target_pairs={{0,3},{1,0},{2,1},{3,2},{4,7},{5,4},{6,5},{7,6},{8,11},{9,8},{10,9... | collective-permute-start | bytes 1179656 | tf_op jit(solution)/shard_map/ppermute | solution.py:19
  265.3 11.6 %copy-start.1 = (bf16[384,384]{1,0:T(8,128)(2,1)S(1)}, bf16[384,384]{1,0:T(8,128)(2,1)}, u32[]{:S(2)}) copy-start(bf16[384,384]{1,0:T(8,128)(2,1)} %copy-done) | copy-start | bytes 884740
  265.3 17.5 %collective-permute-start.17 = (bf16[384,512]{1,0:T(8,128)(2,1)S(1)}, bf16[384,512]{1,0:T(8,128)(2,1)S(1)}, u32[]{:S(2)}, u32[]{:S(2)}) collective-permute-start(bf16[384,512]{1,0:T(8,128)(2,1)S(1)} %convolution_convert_fusion.2), channel_id=1, source_target_pairs={{0,2},{1,3},{2,0},{3,1},{4,6},{5,7},{6,4},{7,5},{8,10},{9,11},{10,... | collective-permute-start | bytes 1179656 | tf_op jit(solution)/shard_map/ppermute | solution.py:19
  270.2 28.0 %collective-permute-start.16 = (bf16[384,512]{1,0:T(8,128)(2,1)S(1)}, bf16[384,512]{1,0:T(8,128)(2,1)S(1)}, u32[]{:S(2)}, u32[]{:S(2)}) collective-permute-start(bf16[384,512]{1,0:T(8,128)(2,1)S(1)} %convolution_convert_fusion.3), channel_id=1, source_target_pairs={{0,3},{1,0},{2,1},{3,2},{4,7},{5,4},{6,5},{7,6},{8,11},{9,8},{10,9... | collective-permute-start | bytes 1179656 | tf_op jit(solution)/shard_map/ppermute | solution.py:19
  273.0 28.4 %collective-permute-start.15 = (bf16[384,512]{1,0:T(8,128)(2,1)S(1)}, bf16[384,512]{1,0:T(8,128)(2,1)S(1)}, u32[]{:S(2)}, u32[]{:S(2)}) collective-permute-start(bf16[384,512]{1,0:T(8,128)(2,1)S(1)} %convolution_convert_fusion.4), channel_id=1, source_target_pairs={{0,1},{1,2},{2,3},{3,0},{4,5},{5,6},{6,7},{7,4},{8,9},{9,10},{10,1... | collective-permute-start | bytes 1179656 | tf_op jit(solution)/shard_map/ppermute | solution.py:19
  277.8 27.3 %collective-permute-start.9 = (bf16[512,384]{1,0:T(8,128)(2,1)S(1)}, bf16[512,384]{1,0:T(8,128)(2,1)S(1)}, u32[]{:S(2)}, u32[]{:S(2)}) collective-permute-start(bf16[512,384]{1,0:T(8,128)(2,1)S(1)} %convolution_convert_fusion.12), channel_id=1, source_target_pairs={{0,1},{1,2},{2,3},{3,0},{4,5},{5,6},{6,7},{7,4},{8,9},{9,10},{10,1... | collective-permute-start | bytes 1179656 | tf_op jit(solution)/shard_map/ppermute | solution.py:19
  282.8 24.5 %collective-permute-start.14 = (bf16[512,384]{1,0:T(8,128)(2,1)S(1)}, bf16[512,384]{1,0:T(8,128)(2,1)S(1)}, u32[]{:S(2)}, u32[]{:S(2)}) collective-permute-start(bf16[512,384]{1,0:T(8,128)(2,1)S(1)} %convolution_convert_fusion.6), channel_id=1, source_target_pairs={{0,2},{1,3},{2,0},{3,1},{4,6},{5,7},{6,4},{7,5},{8,10},{9,11},{10,... | collective-permute-start | bytes 1179656 | tf_op jit(solution)/shard_map/ppermute | solution.py:19
  298.2 16.7 %collective-permute-start.13 = (bf16[512,384]{1,0:T(8,128)(2,1)S(1)}, bf16[512,384]{1,0:T(8,128)(2,1)S(1)}, u32[]{:S(2)}, u32[]{:S(2)}) collective-permute-start(bf16[512,384]{1,0:T(8,128)(2,1)S(1)} %convolution_convert_fusion.7), channel_id=1, source_target_pairs={{0,3},{1,0},{2,1},{3,2},{4,7},{5,4},{6,5},{7,6},{8,11},{9,8},{10,9... | collective-permute-start | bytes 1179656 | tf_op jit(solution)/shard_map/ppermute | solution.py:19
  301.4 13.8 %collective-permute-start.12 = (bf16[512,384]{1,0:T(8,128)(2,1)S(1)}, bf16[512,384]{1,0:T(8,128)(2,1)S(1)}, u32[]{:S(2)}, u32[]{:S(2)}) collective-permute-start(bf16[512,384]{1,0:T(8,128)(2,1)S(1)} %convolution_convert_fusion.8), channel_id=1, source_target_pairs={{0,1},{1,2},{2,3},{3,0},{4,5},{5,6},{6,7},{7,4},{8,9},{9,10},{10,1... | collective-permute-start | bytes 1179656 | tf_op jit(solution)/shard_map/ppermute | solution.py:19
Sparse Core Ops, SparseCore 0:
  10.7 83.7 all-gather.1
  257.5 67.6 reduce-scatter.1
where the time goes:
time: 334 us; the launch traced here: 332 us
  waiting for transfers between devices  138 us (41%)
  starting transfers between devices  81.4 us (24%)
  matrix products  44.4 us (13%)
  blocking collectives  29.2 us (9%)
  local copies, waits for them, and re-layouts  19.6 us (6%)
  between operations  14.7 us (4%)
  other arithmetic  4.4 us (1%)
    ppermute x18, waiting for transfers between devices, shift(): return lax.ppermute(value, 'x', [(i, (i + by) % N_X) for i in range(N_X)])  62.9 us
    ppermute x18, starting transfers between devices, shift(): return lax.ppermute(value, 'x', [(i, (i + by) % N_X) for i in range(N_X)])  58.5 us
    all_gather x1, waiting for transfers between devices, shards(): lax.all_gather(both, 'z', axis=0, tiled=True)  52.2 us
    dot_general x35, matrix products, dot(): lax.dot_general(left, right, (contract, batch), preferred_element_type=F32)  44.4 us
    all_to_all x1, blocking collectives, shards(): lax.all_to_all(row_grad.reshape(-1, slots, cols), PLANE, split_axis=0, co...  29.2 us
    all_to_all x1, starting transfers between devices, plan(): lax.all_to_all(jnp.broadcast_to(mine[None], (N_Z,) + mine.shape), 'z', sp...  15.2 us
    all_to_all x1, waiting for transfers between devices, plan(): lax.all_to_all(jnp.broadcast_to(mine[None], (N_Z,) + mine.shape), 'z', sp...  14.6 us
    dynamic_update_slice x12, local copies, waits for them, and re-layouts, gather_x(): lax.dynamic_update_slice_in_dim(whole, piece[None], (me - by) % N_X, 0)  14.5 us
  transfers between devices with their start and end apart: 22, of which 11 were waited for; matrix products, arithmetic and copies ran while one was open for 9% of the time, Pallas kernels for 0%

commit v1 on v0

--- a/solution.py
+++ b/solution.py
@@ -3,6 +3,7 @@
 from jax import lax
 from jax.sharding import Mesh
 from jax.sharding import PartitionSpec as P
+from jax.lax import all_to_all, axis_size
 
 MOST = 12
 N_Z, N_Y, N_C, N_X = (16, 4, 2, 4)
@@ -67,7 +68,9 @@
     me_z, me_x = (lax.axis_index("z"), lax.axis_index("x"))
     tok, cols = tokens.shape
     both = jnp.concatenate([tokens, grad_out], axis=1)
-    column = lax.all_gather(both, "z", axis=0, tiled=True).reshape(N_X, N_Z // N_X * tok, 2 * cols)
+    column = jnp.concatenate(
+        all_to_all(jnp.stack([both for _ in range(axis_size("z"))], 0), "z", 0, 0), 0
+    ).reshape(N_X, N_Z // N_X * tok, 2 * cols)
     pick, row_gate = plan(routes, gates, me_z)
     full_gate = gather_x(w_gate[0], me_x)
     full_up = gather_x(w_up[0], me_x)

time: 334 us -> 471 us (1.41)
  the two profiles are of different devices: /device:TPU:4 before, /device:TPU:8 now
where the time goes in v1:
time: 471 us; the launch traced here: 469 us
  waiting for transfers between devices  269 us (57%)
  starting transfers between devices  87.9 us (19%)
  matrix products  44.5 us (9%)
  blocking collectives  26.9 us (6%)
  local copies, waits for them, and re-layouts  22.2 us (5%)
  between operations  14.7 us (3%)
    all_to_all x1, waiting for transfers between devices, shards(): all_to_all(jnp.stack([both for _ in range(axis_size('z'))], 0), 'z', 0, 0)  180 us
    ppermute x18, waiting for transfers between devices, shift(): return lax.ppermute(value, 'x', [(i, (i + by) % N_X) for i in range(N_X)])  64.1 us
    ppermute x18, starting transfers between devices, shift(): return lax.ppermute(value, 'x', [(i, (i + by) % N_X) for i in range(N_X)])  60.4 us
    dot_general x35, matrix products, dot(): lax.dot_general(left, right, (contract, batch), preferred_element_type=F32)  44.5 us
    all_to_all x1, blocking collectives, shards(): lax.all_to_all(row_grad.reshape(-1, slots, cols), PLANE, split_axis=0, co...  26.9 us
    all_to_all x1, starting transfers between devices, plan(): lax.all_to_all(jnp.broadcast_to(mine[None], (N_Z,) + mine.shape), 'z', sp...  15.2 us
    dynamic_update_slice x12, local copies, waits for them, and re-layouts, gather_x(): lax.dynamic_update_slice_in_dim(whole, piece[None], (me - by) % N_X, 0)  14.6 us
    all_to_all x1, waiting for transfers between devices, plan(): lax.all_to_all(jnp.broadcast_to(mine[None], (N_Z,) + mine.shape), 'z', sp...  13.7 us
  transfers between devices with their start and end apart: 22, of which 12 were waited for; matrix products, arithmetic and copies ran while one was open for 6% of the time, Pallas kernels for 0%

profile of v1, /device:TPU:8, one launch (start us, length us, event | category | flops | bytes accessed | tf_op | source)
XLA Modules:
  0.0 468.5 jit_solution(3113845418202620086)
XLA Ops:
  9.2 15.2 %all-to-all-start = ((f32[16,16,128]{2,1,0:T(8,128)}), f32[16,16,128]{2,1,0:T(8,128)S(1)}, u32[]{:S(2)}, u32[]{:S(2)}) async-start(f32[16,16,128]{2,1,0:T(8,128)} %broadcast_in_dim.103), calls=%async_computation | async-start | bytes 262144 | tf_op jit(solution)/shard_map/all_to_all | solution.py:34
  25.4 13.7 %all-to-all-done = f32[16,16,128]{2,1,0:T(8,128)S(1)} async-done(((f32[16,16,128]{2,1,0:T(8,128)}), f32[16,16,128]{2,1,0:T(8,128)S(1)}, u32[]{:S(2)}, u32[]{:S(2)}) %all-to-all-start) | async-done | bytes 131104 | tf_op jit(solution)/shard_map/all_to_all | solution.py:34
  39.1 2.6 stack.12
  41.7 4.6 all-to-all-start.1
  47.8 179.5 %all-to-all-done.1 = bf16[16,128,1024]{2,1,0:T(8,128)(2,1)} async-done(((bf16[16,128,1024]{2,1,0:T(8,128)(2,1)}), bf16[16,128,1024]{2,1,0:T(8,128)(2,1)}, u32[]{:S(2)}, u32[]{:S(2)}) %all-to-all-start.1) | async-done | bytes 4194336 | tf_op jit(solution)/shard_map/all_to_all | solution.py:72
  227.3 5.7 %multiply_convert_fusion = bf16[4,384,1024]{2,1,0:T(8,128)(2,1)} fusion(f32[4,384]{1,0:T(4,128)S(1)} %broadcast_in_dim.112, pred[1024]{0:T(1024)(128)(4,1)S(1)} %iota_compare_fusion.1, pred[4,384,512]{2,1,0:T(32,128)(4,1)S(1)} %bitcast_compare_fusion, bf16[4,512,1024]{2,1,0:T(8,128)(2,1)} %bitcast.7), kind=kOutput, calls=%fused_computation | convolution fusion | flops 1615331328 | bytes 8133632 | tf_op jit(solution)/shard_map/dot_general | solution.py:16
  233.0 7.7 %all-to-all-start.2 = ((bf16[32,48,1024]{2,1,0:T(8,128)(2,1)}), bf16[32,48,1024]{2,1,0:T(8,128)(2,1)S(1)}, u32[]{:S(2)}, u32[]{:S(2)}) async-start(bf16[32,48,1024]{2,1,0:T(8,128)(2,1)} %bitcast.213), calls=%async_computation.2 | async-start | bytes 6291456 | tf_op jit(solution)/shard_map/all_to_all | solution.py:83
  240.7 3.4 collective-permute-start.6
  244.1 4.6 collective-permute-start.7
  248.7 3.3 collective-permute-start.8
  252.1 2.5 collective-permute-start
  254.6 2.8 collective-permute-start.1
  263.8 23.5 %collective-permute-done.6 = bf16[512,384]{1,0:T(8,128)(2,1)} collective-permute-done((bf16[512,384]{1,0:T(8,128)(2,1)S(1)}, bf16[512,384]{1,0:T(8,128)(2,1)}, u32[]{:S(2)}, u32[]{:S(2)}) %collective-permute-start.6) | collective-permute-done | bytes 393248 | tf_op jit(solution)/shard_map/ppermute | solution.py:20
  287.2 4.4 collective-permute-start.2
  293.4 10.2 %collective-permute-done = bf16[384,512]{1,0:T(8,128)(2,1)} collective-permute-done((bf16[384,512]{1,0:T(8,128)(2,1)}, bf16[384,512]{1,0:T(8,128)(2,1)}, u32[]{:S(2)}, u32[]{:S(2)}) %collective-permute-start) | collective-permute-done | bytes 393248 | tf_op jit(solution)/shard_map/ppermute | solution.py:20
  303.6 2.4 collective-permute-start.3
  307.8 5.8 %collective-permute-start.4 = (bf16[512,384]{1,0:T(8,128)(2,1)S(1)}, bf16[512,384]{1,0:T(8,128)(2,1)S(1)}, u32[]{:S(2)}, u32[]{:S(2)}) collective-permute-start(bf16[512,384]{1,0:T(8,128)(2,1)S(1)} %bitcast.223), channel_id=1, source_target_pairs={{0,2},{1,3},{2,0},{3,1},{4,6},{5,7},{6,4},{7,5},{8,10},{9,11},{10,... | collective-permute-start | bytes 1179656 | tf_op jit(solution)/shard_map/ppermute | solution.py:20
  315.5 2.3 collective-permute-start.5
  323.6 7.2 %collective-permute-done.4 = bf16[512,384]{1,0:T(8,128)(2,1)S(1)} collective-permute-done((bf16[512,384]{1,0:T(8,128)(2,1)S(1)}, bf16[512,384]{1,0:T(8,128)(2,1)S(1)}, u32[]{:S(2)}, u32[]{:S(2)}) %collective-permute-start.4) | collective-permute-done | bytes 393248 | tf_op jit(solution)/shard_map/ppermute | solution.py:20
  347.6 2.3 multiply_convert_fusion.1
  361.4 26.9 %all_to_all.20 = bf16[32,48,512]{2,1,0:T(8,128)(2,1)S(1)} all-to-all(bf16[32,48,512]{2,1,0:T(8,128)(2,1)S(1)} %bitcast.211), channel_id=1, replica_groups=mesh['z'=16,'y'=4,'c'=2,'x'=4] {'x','y','c'}, dimensions={0} | all-to-all | bytes 3145728 | tf_op jit(solution)/shard_map/all_to_all | solution.py:109
  388.3 2.6 convolution_convert_fusion
  391.8 3.2 collective-permute-start.11
  395.5 3.5 collective-permute-start.10
  399.4 3.2 collective-permute-start.17
  402.9 3.9 collective-permute-start.16
  410.6 2.8 collective-permute-start.9
  415.6 4.0 collective-permute-start.14
  419.6 11.3 %collective-permute-done.16 = bf16[384,512]{1,0:T(8,128)(2,1)S(1)} collective-permute-done((bf16[384,512]{1,0:T(8,128)(2,1)S(1)}, bf16[384,512]{1,0:T(8,128)(2,1)S(1)}, u32[]{:S(2)}, u32[]{:S(2)}) %collective-permute-start.16) | collective-permute-done | bytes 393248 | tf_op jit(solution)/shard_map/ppermute | solution.py:20
  430.9 4.4 collective-permute-start.13
  440.9 6.6 %collective-permute-done.13 = bf16[512,384]{1,0:T(8,128)(2,1)S(1)} collective-permute-done((bf16[512,384]{1,0:T(8,128)(2,1)S(1)}, bf16[512,384]{1,0:T(8,128)(2,1)S(1)}, u32[]{:S(2)}, u32[]{:S(2)}) %collective-permute-start.13) | collective-permute-done | bytes 393248 | tf_op jit(solution)/shard_map/ppermute | solution.py:20
  450.5 11.2 %reduce-scatter.2.cloned.1.call-done = bf16[128,512]{1,0:T(8,128)(2,1)} async-done(((bf16[2048,512]{1,0:T(8,128)(2,1)}), bf16[128,512]{1,0:T(8,128)(2,1)}) %reduce-scatter.2.cloned.1.call-update) | async-done | bytes 131088 | tf_op jit(solution)/shard_map/reduce_scatter | solution.py:113
  (100 shorter events, 66.4 us)
Async XLA Ops:
  9.2 29.9 %all-to-all-start = ((f32[16,16,128]{2,1,0:T(8,128)}), f32[16,16,128]{2,1,0:T(8,128)S(1)}, u32[]{:S(2)}, u32[]{:S(2)}) async-start(f32[16,16,128]{2,1,0:T(8,128)} %broadcast_in_dim.103), calls=%async_computation | async-start | bytes 262144 | tf_op jit(solution)/shard_map/all_to_all | solution.py:34
  41.7 185.6 %all-to-all-start.1 = ((bf16[16,128,1024]{2,1,0:T(8,128)(2,1)}), bf16[16,128,1024]{2,1,0:T(8,128)(2,1)}, u32[]{:S(2)}, u32[]{:S(2)}) async-start(bf16[16,128,1024]{2,1,0:T(8,128)(2,1)} %stack.12), calls=%async_computation.1 | async-start | bytes 8388608 | tf_op jit(solution)/shard_map/all_to_all | solution.py:72
  47.2 185.8 %copy-start.3 = (pred[4,384,512]{2,1,0:T(32,128)(4,1)}, pred[4,384,512]{2,1,0:T(32,128)(4,1)S(1)}, u32[]{:S(2)}) copy-start(pred[4,384,512]{2,1,0:T(32,128)(4,1)S(1)} %bitcast_compare_fusion) | copy-start | bytes 2359300
  233.0 7.7 %copy-start.5 = (bf16[1,512,384]{2,1,0:T(8,128)(2,1)S(1)}, bf16[1,512,384]{2,1,0:T(8,128)(2,1)}, u32[]{:S(2)}) copy-start(bf16[1,512,384]{2,1,0:T(8,128)(2,1)} %param.11) | copy-start | bytes 1179652
  233.0 99.5 %all-to-all-start.2 = ((bf16[32,48,1024]{2,1,0:T(8,128)(2,1)}), bf16[32,48,1024]{2,1,0:T(8,128)(2,1)S(1)}, u32[]{:S(2)}, u32[]{:S(2)}) async-start(bf16[32,48,1024]{2,1,0:T(8,128)(2,1)} %bitcast.213), calls=%async_computation.2 | async-start | bytes 6291456 | tf_op jit(solution)/shard_map/all_to_all | solution.py:83
  240.7 221.0 %reduce-scatter.2.cloned.1.call-start = ((), (), s32[]{:S(2)}) async-start(), calls=%async_computation.5 | async-start | bytes 2228224 | tf_op jit(solution)/shard_map/reduce_scatter | solution.py:113
  240.7 46.5 %collective-permute-start.6 = (bf16[512,384]{1,0:T(8,128)(2,1)S(1)}, bf16[512,384]{1,0:T(8,128)(2,1)}, u32[]{:S(2)}, u32[]{:S(2)}) collective-permute-start(bf16[512,384]{1,0:T(8,128)(2,1)S(1)} %bitcast.216), channel_id=1, source_target_pairs={{0,1},{1,2},{2,3},{3,0},{4,5},{5,6},{6,7},{7,4},{8,9},{9,10},{10,1... | collective-permute-start | bytes 1179656 | tf_op jit(solution)/shard_map/ppermute | solution.py:20
  244.1 63.7 %collective-permute-start.7 = (bf16[512,384]{1,0:T(8,128)(2,1)S(1)}, bf16[512,384]{1,0:T(8,128)(2,1)}, u32[]{:S(2)}, u32[]{:S(2)}) collective-permute-start(bf16[512,384]{1,0:T(8,128)(2,1)S(1)} %bitcast.217), channel_id=1, source_target_pairs={{0,2},{1,3},{2,0},{3,1},{4,6},{5,7},{6,4},{7,5},{8,10},{9,11},{10,... | collective-permute-start | bytes 1179656 | tf_op jit(solution)/shard_map/ppermute | solution.py:20
  248.7 70.8 %collective-permute-start.8 = (bf16[512,384]{1,0:T(8,128)(2,1)S(1)}, bf16[512,384]{1,0:T(8,128)(2,1)}, u32[]{:S(2)}, u32[]{:S(2)}) collective-permute-start(bf16[512,384]{1,0:T(8,128)(2,1)S(1)} %bitcast.218), channel_id=1, source_target_pairs={{0,3},{1,0},{2,1},{3,2},{4,7},{5,4},{6,5},{7,6},{8,11},{9,8},{10,9... | collective-permute-start | bytes 1179656 | tf_op jit(solution)/shard_map/ppermute | solution.py:20
  252.1 51.6 %collective-permute-start = (bf16[384,512]{1,0:T(8,128)(2,1)}, bf16[384,512]{1,0:T(8,128)(2,1)}, u32[]{:S(2)}, u32[]{:S(2)}) collective-permute-start(bf16[384,512]{1,0:T(8,128)(2,1)} %bitcast.219), channel_id=1, source_target_pairs={{0,1},{1,2},{2,3},{3,0},{4,5},{5,6},{6,7},{7,4},{8,9},{9,10},{10,1... | collective-permute-start | bytes 1179656 | tf_op jit(solution)/shard_map/ppermute | solution.py:20
  254.6 60.9 %collective-permute-start.1 = (bf16[384,512]{1,0:T(8,128)(2,1)}, bf16[384,512]{1,0:T(8,128)(2,1)}, u32[]{:S(2)}, u32[]{:S(2)}) collective-permute-start(bf16[384,512]{1,0:T(8,128)(2,1)} %bitcast.220), channel_id=1, source_target_pairs={{0,2},{1,3},{2,0},{3,1},{4,6},{5,7},{6,4},{7,5},{8,10},{9,11},{10,... | collective-permute-start | bytes 1179656 | tf_op jit(solution)/shard_map/ppermute | solution.py:20
  258.7 2.1 copy-start.6
  261.6 1.4 copy-start.8
  261.6 25.6 %copy-start.7 = (bf16[1,384,512]{2,1,0:T(8,128)(2,1)S(1)}, bf16[1,384,512]{2,1,0:T(8,128)(2,1)}, u32[]{:S(2)}) copy-start(bf16[1,384,512]{2,1,0:T(8,128)(2,1)} %param.13) | copy-start | bytes 1179652
  287.2 34.1 %collective-permute-start.2 = (bf16[384,512]{1,0:T(8,128)(2,1)S(1)}, bf16[384,512]{1,0:T(8,128)(2,1)S(1)}, u32[]{:S(2)}, u32[]{:S(2)}) collective-permute-start(bf16[384,512]{1,0:T(8,128)(2,1)S(1)} %bitcast.221), channel_id=1, source_target_pairs={{0,3},{1,0},{2,1},{3,2},{4,7},{5,4},{6,5},{7,6},{8,11},{9,8},{10,9... | collective-permute-start | bytes 1179656 | tf_op jit(solution)/shard_map/ppermute | solution.py:20
  303.6 19.1 %collective-permute-start.3 = (bf16[512,384]{1,0:T(8,128)(2,1)S(1)}, bf16[512,384]{1,0:T(8,128)(2,1)S(1)}, u32[]{:S(2)}, u32[]{:S(2)}) collective-permute-start(bf16[512,384]{1,0:T(8,128)(2,1)S(1)} %bitcast.222), channel_id=1, source_target_pairs={{0,1},{1,2},{2,3},{3,0},{4,5},{5,6},{6,7},{7,4},{8,9},{9,10},{10,1... | collective-permute-start | bytes 1179656 | tf_op jit(solution)/shard_map/ppermute | solution.py:20
  307.8 23.0 %collective-permute-start.4 = (bf16[512,384]{1,0:T(8,128)(2,1)S(1)}, bf16[512,384]{1,0:T(8,128)(2,1)S(1)}, u32[]{:S(2)}, u32[]{:S(2)}) collective-permute-start(bf16[512,384]{1,0:T(8,128)(2,1)S(1)} %bitcast.223), channel_id=1, source_target_pairs={{0,2},{1,3},{2,0},{3,1},{4,6},{5,7},{6,4},{7,5},{8,10},{9,11},{10,... | collective-permute-start | bytes 1179656 | tf_op jit(solution)/shard_map/ppermute | solution.py:20
  315.5 16.1 %collective-permute-start.5 = (bf16[512,384]{1,0:T(8,128)(2,1)S(1)}, bf16[512,384]{1,0:T(8,128)(2,1)S(1)}, u32[]{:S(2)}, u32[]{:S(2)}) collective-permute-start(bf16[512,384]{1,0:T(8,128)(2,1)S(1)} %bitcast.224), channel_id=1, source_target_pairs={{0,3},{1,0},{2,1},{3,2},{4,7},{5,4},{6,5},{7,6},{8,11},{9,8},{10,9... | collective-permute-start | bytes 1179656 | tf_op jit(solution)/shard_map/ppermute | solution.py:20
  349.9 4.3 copy-start
  361.4 26.9 %copy-start.4 = (pred[4,384,512]{2,1,0:T(32,128)(4,1)S(1)}, pred[4,384,512]{2,1,0:T(32,128)(4,1)}, u32[]{:S(2)}) copy-start(pred[4,384,512]{2,1,0:T(32,128)(4,1)} %copy-done.3) | copy-start | bytes 2359300
  391.3 7.6 %copy-start.2 = (bf16[384,384]{1,0:T(8,128)(2,1)S(1)}, bf16[384,384]{1,0:T(8,128)(2,1)}, u32[]{:S(2)}) copy-start(bf16[384,384]{1,0:T(8,128)(2,1)} %get-tuple-element.8) | copy-start | bytes 884740
  391.8 18.8 %collective-permute-start.11 = (bf16[512,384]{1,0:T(8,128)(2,1)S(1)}, bf16[512,384]{1,0:T(8,128)(2,1)S(1)}, u32[]{:S(2)}, u32[]{:S(2)}) collective-permute-start(bf16[512,384]{1,0:T(8,128)(2,1)S(1)} %convolution_convert_fusion.10), channel_id=1, source_target_pairs={{0,2},{1,3},{2,0},{3,1},{4,6},{5,7},{6,4},{7,5},{8,10},{9,11},{10,... | collective-permute-start | bytes 1179656 | tf_op jit(solution)/shard_map/ppermute | solution.py:20
  395.5 43.0 %collective-permute-start.10 = (bf16[512,384]{1,0:T(8,128)(2,1)S(1)}, bf16[512,384]{1,0:T(8,128)(2,1)S(1)}, u32[]{:S(2)}, u32[]{:S(2)}) collective-permute-start(bf16[512,384]{1,0:T(8,128)(2,1)S(1)} %convolution_convert_fusion.11), channel_id=1, source_target_pairs={{0,3},{1,0},{2,1},{3,2},{4,7},{5,4},{6,5},{7,6},{8,11},{9,8},{10,9... | collective-permute-start | bytes 1179656 | tf_op jit(solution)/shard_map/ppermute | solution.py:20
  399.3 10.3 %copy-start.1 = (bf16[384,384]{1,0:T(8,128)(2,1)S(1)}, bf16[384,384]{1,0:T(8,128)(2,1)}, u32[]{:S(2)}) copy-start(bf16[384,384]{1,0:T(8,128)(2,1)} %copy-done) | copy-start | bytes 884740
  399.4 16.2 %collective-permute-start.17 = (bf16[384,512]{1,0:T(8,128)(2,1)S(1)}, bf16[384,512]{1,0:T(8,128)(2,1)S(1)}, u32[]{:S(2)}, u32[]{:S(2)}) collective-permute-start(bf16[384,512]{1,0:T(8,128)(2,1)S(1)} %convolution_convert_fusion.2), channel_id=1, source_target_pairs={{0,2},{1,3},{2,0},{3,1},{4,6},{5,7},{6,4},{7,5},{8,10},{9,11},{10,... | collective-permute-start | bytes 1179656 | tf_op jit(solution)/shard_map/ppermute | solution.py:20
  402.9 28.0 %collective-permute-start.16 = (bf16[384,512]{1,0:T(8,128)(2,1)S(1)}, bf16[384,512]{1,0:T(8,128)(2,1)S(1)}, u32[]{:S(2)}, u32[]{:S(2)}) collective-permute-start(bf16[384,512]{1,0:T(8,128)(2,1)S(1)} %convolution_convert_fusion.3), channel_id=1, source_target_pairs={{0,3},{1,0},{2,1},{3,2},{4,7},{5,4},{6,5},{7,6},{8,11},{9,8},{10,9... | collective-permute-start | bytes 1179656 | tf_op jit(solution)/shard_map/ppermute | solution.py:20
  407.3 28.0 %collective-permute-start.15 = (bf16[384,512]{1,0:T(8,128)(2,1)S(1)}, bf16[384,512]{1,0:T(8,128)(2,1)S(1)}, u32[]{:S(2)}, u32[]{:S(2)}) collective-permute-start(bf16[384,512]{1,0:T(8,128)(2,1)S(1)} %convolution_convert_fusion.4), channel_id=1, source_target_pairs={{0,1},{1,2},{2,3},{3,0},{4,5},{5,6},{6,7},{7,4},{8,9},{9,10},{10,1... | collective-permute-start | bytes 1179656 | tf_op jit(solution)/shard_map/ppermute | solution.py:20
  410.6 27.8 %collective-permute-start.9 = (bf16[512,384]{1,0:T(8,128)(2,1)S(1)}, bf16[512,384]{1,0:T(8,128)(2,1)S(1)}, u32[]{:S(2)}, u32[]{:S(2)}) collective-permute-start(bf16[512,384]{1,0:T(8,128)(2,1)S(1)} %convolution_convert_fusion.12), channel_id=1, source_target_pairs={{0,1},{1,2},{2,3},{3,0},{4,5},{5,6},{6,7},{7,4},{8,9},{9,10},{10,1... | collective-permute-start | bytes 1179656 | tf_op jit(solution)/shard_map/ppermute | solution.py:20
  415.6 25.3 %collective-permute-start.14 = (bf16[512,384]{1,0:T(8,128)(2,1)S(1)}, bf16[512,384]{1,0:T(8,128)(2,1)S(1)}, u32[]{:S(2)}, u32[]{:S(2)}) collective-permute-start(bf16[512,384]{1,0:T(8,128)(2,1)S(1)} %convolution_convert_fusion.6), channel_id=1, source_target_pairs={{0,2},{1,3},{2,0},{3,1},{4,6},{5,7},{6,4},{7,5},{8,10},{9,11},{10,... | collective-permute-start | bytes 1179656 | tf_op jit(solution)/shard_map/ppermute | solution.py:20
  430.9 16.6 %collective-permute-start.13 = (bf16[512,384]{1,0:T(8,128)(2,1)S(1)}, bf16[512,384]{1,0:T(8,128)(2,1)S(1)}, u32[]{:S(2)}, u32[]{:S(2)}) collective-permute-start(bf16[512,384]{1,0:T(8,128)(2,1)S(1)} %convolution_convert_fusion.7), channel_id=1, source_target_pairs={{0,3},{1,0},{2,1},{3,2},{4,7},{5,4},{6,5},{7,6},{8,11},{9,8},{10,9... | collective-permute-start | bytes 1179656 | tf_op jit(solution)/shard_map/ppermute | solution.py:20
  435.3 13.9 %collective-permute-start.12 = (bf16[512,384]{1,0:T(8,128)(2,1)S(1)}, bf16[512,384]{1,0:T(8,128)(2,1)S(1)}, u32[]{:S(2)}, u32[]{:S(2)}) collective-permute-start(bf16[512,384]{1,0:T(8,128)(2,1)S(1)} %convolution_convert_fusion.8), channel_id=1, source_target_pairs={{0,1},{1,2},{2,3},{3,0},{4,5},{5,6},{6,7},{7,4},{8,9},{9,10},{10,1... | collective-permute-start | bytes 1179656 | tf_op jit(solution)/shard_map/ppermute | solution.py:20
Sparse Core Ops, SparseCore 0:
  391.1 70.5 reduce-scatter.1
